TPU v7x, 32 devices: a whole 2x2x4 slice. The times are simulated.
32 devices in a mesh: grp: 4 (over x, core), seq: 8 (over z, y).
Axes of the slice: x: 2, y: 2, z: 4, core: 2. Of those that a mesh axis runs over, the one named last changes fastest.
Arguments:
- queries: bfloat16 [4096, 512], P(('grp', 'seq')), may hold values from -4.5 to 5.5
- key_vectors: bfloat16 [4096, 512], P(('grp', 'seq')), may hold values from -4.5 to 5.5
- value_vectors: bfloat16 [4096, 1024], P(('grp', 'seq')), may hold values from -6 to 6
- input_gate: float32 [4, 4096], P(None, ('grp', 'seq')), may hold values from -4 to 114
- forget_gate: float32 [4, 4096], P(None, ('grp', 'seq')), may hold values from -3 to 25
Outputs:
- hidden_states: bfloat16 [4096, 1024], P(('grp', 'seq'))
All inputs are finite; a program needn't handle non-finite values.
Results may differ from a plain program's by a relative error of at most 0.028.
Values sent between devices are 32-bit elements; how exact they have to be, the bound alone decides.
No kernel may reach another device: no remote copies, remote signals or barrier semaphores. Data moves between devices by JAX's collectives and lax.ppermute only.
A program may use at most 64 MiB of HBM per device.

v0:
```python
import jax
import jax.numpy as jnp
from jax import lax
from jax.sharding import PartitionSpec as P

exact_precision_mode = lax.Precision.HIGHEST
floor_value = -1e30


def prefix_2(value, axis, join, neutral, backward):
    count, mine = (lax.axis_size(axis), lax.axis_index(axis))
    pieces = jax.tree.map(lambda part: lax.all_gather(part, axis), value)
    if backward:
        pieces = jax.tree.map(lambda part: part[::-1], pieces)
        mine = count - 1 - mine
    subtotal = jax.tree.map(
        lambda part, zero: jnp.full_like(part, 0) + jnp.asarray(zero, part.dtype), value, neutral
    )

    def lap(position, subtotal):
        longer = join(subtotal, jax.tree.map(lambda part: part[position], pieces))
        return jax.tree.map(lambda new, old: jnp.where(position < mine, new, old), longer, subtotal)

    return lax.fori_loop(0, count - 1, lap, subtotal)


def combine_states(earlier, later):
    early_matrix, early_vector, early_top, early_decay = earlier
    late_matrix, late_vector, late_top, late_decay = later
    joined = jnp.maximum(early_top + late_decay, late_top)
    early_weight = jnp.exp(early_top + late_decay - joined)
    late_weight = jnp.exp(late_top - joined)
    new_matrix = (
        early_weight[..., None, None] * early_matrix + late_weight[..., None, None] * late_matrix
    )
    new_vector = early_weight[..., None] * early_vector + late_weight[..., None] * late_vector
    return (new_matrix, new_vector, joined, early_decay + late_decay)


def combine_backward(higher, lower):
    return combine_states(lower, higher)


def on_device(queries, key_vectors, value_vectors, input_gate, forget_gate):
    head_count = input_gate.shape[0]
    length = queries.shape[0]
    key_dim = queries.shape[1] // head_count
    value_dim = value_vectors.shape[1] // head_count
    query_scaling = key_dim ** (-0.5)
    cumulative = jnp.cumsum(jax.nn.log_sigmoid(forget_gate), axis=1)
    block_decay = cumulative[:, -1]
    weight_log = block_decay[:, None] - cumulative + input_gate
    block_top = jnp.max(weight_log, axis=1)
    weight_tensor = jnp.exp(weight_log - block_top[:, None])
    keys_widened = key_vectors.astype(jnp.float32).reshape(length, head_count, key_dim)
    values_widened = (
        value_vectors.astype(jnp.float32).reshape(length, head_count, value_dim)
        * weight_tensor.T[:, :, None]
    )
    memory_matrix = jnp.einsum(
        "fji,fjb->jib", keys_widened, values_widened, precision=exact_precision_mode
    )
    vector = jnp.einsum("shk,hs->hk", keys_widened, weight_tensor, precision=exact_precision_mode)
    local_state = (memory_matrix, vector, block_top, block_decay)
    identity = (
        jnp.zeros_like(memory_matrix),
        jnp.zeros_like(vector),
        jnp.full_like(block_top, floor_value),
        jnp.zeros_like(block_decay),
    )
    within = prefix_2(local_state, "seq", combine_states, identity, False)
    through = combine_states(within, local_state)
    later_part = prefix_2(local_state, "seq", combine_backward, identity, True)
    group_state = combine_states(through, later_part)
    before = prefix_2(group_state, "grp", combine_states, identity, False)
    prefix = combine_states(before, within)
    previous_memory_matrix, prev_vector, prev_top, prev_decay = prefix
    rows = lax.broadcasted_iota(jnp.int32, (length, length), 0)
    cols = lax.broadcasted_iota(jnp.int32, (length, length), 1)
    causal = rows >= cols
    pieces = []
    for head_index in range(head_count):
        query_head = queries[:, head_index * key_dim : (head_index + 1) * key_dim]
        key_head = key_vectors[:, head_index * key_dim : (head_index + 1) * key_dim]
        value_head = value_vectors[:, head_index * value_dim : (head_index + 1) * value_dim]
        scores = (
            jnp.einsum("tk,sk->ts", query_head, key_head, preferred_element_type=jnp.float32)
            * query_scaling
        )
        head_cumul = cumulative[head_index]
        log_decay = head_cumul[:, None] - head_cumul[None, :] + input_gate[head_index][None, :]
        log_decay = jnp.where(causal, log_decay, -jnp.inf)
        row_top = jnp.max(log_decay, axis=1)
        weighted = jnp.exp(log_decay - row_top[:, None]) * scores
        inner_den = jnp.sum(weighted, axis=1)
        inner_num = jnp.dot(
            weighted.astype(jnp.bfloat16), value_head, preferred_element_type=jnp.float32
        )
        head_top = prev_top[head_index]
        stab = jnp.maximum(head_cumul + head_top, row_top)
        inner_factor = jnp.exp(row_top - stab)
        outer_factor = jnp.exp(head_cumul + head_top - stab)
        query_widened = query_head.astype(jnp.float32)
        carried_numerator = (
            jnp.dot(
                query_widened, previous_memory_matrix[head_index], precision=exact_precision_mode
            )
            * query_scaling
        )
        carried_den = (
            jnp.dot(query_widened, prev_vector[head_index], precision=exact_precision_mode)
            * query_scaling
        )
        numer = inner_factor[:, None] * inner_num + outer_factor[:, None] * carried_numerator
        denom = inner_factor * inner_den + outer_factor * carried_den
        output = numer / jnp.maximum(jnp.abs(denom), jnp.exp(-stab))[:, None]
        pieces.append(output.astype(jnp.bfloat16))
    return jnp.concatenate(pieces, axis=1)


def solution(mesh):
    return jax.shard_map(
        on_device,
        mesh=mesh,
        in_specs=(
            P(("grp", "seq"), None),
            P(("grp", "seq"), None),
            P(("grp", "seq"), None),
            P(None, ("grp", "seq")),
            P(None, ("grp", "seq")),
        ),
        out_specs=P(("grp", "seq"), None),
        check_vma=False,
    )
```

profile of v0, /device:TPU:0, one launch (start us, length us, event | category | flops | bytes accessed | tf_op | source)
XLA Modules:
  0.0 155.3 jit_solution(9596271356633148863)
XLA Ops:
  6.5 0.7 fusion.96
  7.2 0.3 reduce_window_sum.11
  7.7 0.9 fusion.105
  8.6 0.8 subtract_exponential_fusion.6
  9.4 1.1 copy.44
  10.5 1.3 convolution_bitcast_fusion
  11.7 1.0 copy.30
  12.9 1.2 dynamic-slice
  14.7 0.2 dynamic-update-slice.1
  15.1 23.3 %all-reduce.4 = (f32[32]{0:T(128)S(1)}, f32[32]{0:T(128)S(1)}) all-reduce(f32[32]{0:T(128)S(1)} %dynamic-update-slice.1, f32[32]{0:T(128)S(1)} %dynamic-update-slice), channel_id=3, replica_groups=mesh['grp'=4,'seq'=8] {'seq'}, use_global_device_ids=true, to_apply=%add.1 | all-reduce | flops 64 | bytes 512
  38.6 1.1 fusion.63
  39.7 26.3 %all-gather.8 = f32[8,4,128]{2,1,0:T(4,128)S(1)} all-gather(f32[1,4,128]{2,1,0:T(4,128)S(1)} %bitcast.284), channel_id=5, replica_groups=mesh['grp'=4,'seq'=8] {'seq'}, dimensions={0}, use_global_device_ids=true | all-gather | bytes 18432 | tf_op jit(solution)/shard_map/all_gather | solution.py:12
  66.1 1.2 dynamic-slice.2
  67.8 21.5 %all-gather.13.cloned.1.call-done = f32[32,128,256]{2,1,0:T(8,128)} async-done(((f32[4,128,256]{2,1,0:T(8,128)}), f32[32,128,256]{2,1,0:T(8,128)}) %all-gather.13.cloned.1.call-update) | async-done | bytes 4194320 | tf_op jit(solution)/shard_map/all_gather | solution.py:12
  89.4 4.6 %rev.13 = f32[8,4,128,256]{3,2,1,0:T(8,128)} reverse(f32[8,4,128,256]{3,2,1,0:T(8,128)} %bitcast.278), dimensions={0} | reverse | bytes 8388608 | tf_op jit(solution)/shard_map/rev | solution.py:14
  94.0 9.2 %while.58 = (s32[]{:T(128)}, f32[4,128,256]{2,1,0:T(8,128)S(1)}, f32[4,128]{1,0:T(4,128)S(1)}, f32[4]{0:T(128)S(1)}, f32[4]{0:T(128)S(1)}, /*index=5*/s32[]{:T(1...) while((s32[]{:T(128)}, f32[4,128,256]{2,1,0:T(8,128)S(1)}, ...), condition=%wide.region_4.5_spmd.clone, body=%wide.region_3.4_spmd.clone.sunk | while | flops 657964 | bytes 1579405 | solution.py:24
  94.0 1.2 fusion.127
  95.3 1.2 fusion.127
  96.7 1.2 fusion.127
  98.0 1.2 fusion.127
  99.3 1.2 fusion.127
  100.6 1.2 fusion.127
  101.9 1.2 fusion.127
  103.2 9.2 %while.59 = (s32[]{:T(128)}, f32[4,128,256]{2,1,0:T(8,128)S(1)}, f32[4,128]{1,0:T(4,128)S(1)}, f32[4]{0:T(128)S(1)}, f32[4]{0:T(128)S(1)}, /*index=5*/s32[]{:T(1...) while((s32[]{:T(128)}, f32[4,128,256]{2,1,0:T(8,128)S(1)}, ...), condition=%wide.region_6.7_spmd.clone, body=%wide.region_5.6_spmd.clone.sunk | while | flops 657968 | bytes 1579434 | solution.py:24
  103.2 1.2 fusion.129
  104.5 1.2 fusion.129
  105.9 1.2 fusion.129
  107.2 1.2 fusion.129
  108.5 1.2 fusion.129
  109.8 1.2 fusion.129
  111.1 1.2 fusion.129
  113.2 1.0 copy.33
  115.3 5.7 %all-reduce.5 = (f32[16]{0:T(128)S(1)}, f32[16]{0:T(128)S(1)}) all-reduce(f32[16]{0:T(128)S(1)} %get-tuple-element.756, f32[16]{0:T(128)S(1)} %get-tuple-element.758), channel_id=6, replica_groups=mesh['grp'=4,'seq'=8] {'grp'}, use_global_device_ids=true, to_apply=%add.2 | all-reduce | flops 32 | bytes 256
  121.3 5.2 %all-gather.9 = f32[4,4,128]{2,1,0:T(4,128)S(1)} all-gather(f32[1,4,128]{2,1,0:T(4,128)S(1)} %add_bitcast_fusion), channel_id=9, replica_groups=mesh['grp'=4,'seq'=8] {'grp'}, dimensions={0}, use_global_device_ids=true | all-gather | bytes 10240 | tf_op jit(solution)/shard_map/all_gather | solution.py:12
  126.4 8.9 %all-gather.15.cloned.1.call-done = f32[16,128,256]{2,1,0:T(8,128)} async-done(((f32[4,128,256]{2,1,0:T(8,128)}), f32[16,128,256]{2,1,0:T(8,128)}) %all-gather.15.cloned.1.call-update) | async-done | bytes 2097168 | tf_op jit(solution)/shard_map/all_gather | solution.py:12
  135.3 4.0 %while.60 = (s32[]{:T(128)}, f32[4,128,256]{2,1,0:T(8,128)S(1)}, f32[4,128]{1,0:T(4,128)S(1)}, f32[4]{0:T(128)S(1)}, s32[]{:T(128)}, /*index=5*/f32[4,4]{1,0:T(4...) while((s32[]{:T(128)}, f32[4,128,256]{2,1,0:T(8,128)S(1)}, ...), condition=%wide.region_8.9_spmd.clone, body=%wide.region_7.8_spmd.clone.sunk | while | flops 657952 | bytes 1579365 | solution.py:24
  135.4 1.2 fusion.131
  136.7 1.2 fusion.131
  138.0 1.2 fusion.131
  139.3 0.7 fusion.109
  140.2 0.8 fusion.48
  141.0 0.7 fusion.52
  141.7 2.6 %broadcast_multiply_fusion.3 = (f32[128]{0:T(128)S(1)}, f32[128]{0:T(128)S(1)}, f32[128]{0:T(128)S(1)}, f32[128]{0:T(128)S(1)}, f32[128]{0:T(128)S(1)}, /*index=...) fusion(f32[]{:T(128)} %bitcast.15, f32[128]{0:T(128)S(1)} %get-tuple-element.774, f32[4,128]{1,0:T(4,128)S(1)} %reduce_window_sum.11, ...), kind=kLoop, calls=%fused_computation.198 | loop fusion | flops 2560 | bytes 8208 | tf_op jit(solution)/shard_map/mul | solution.py:114
  144.3 0.8 fusion.56
  145.1 0.8 fusion.60
  146.0 0.3 convolution_multiply_fusion.7
  146.8 0.2 fusion.36
  147.7 0.7 pad_maximum_fusion
  (118 shorter events, 6.1 us)
Async XLA Ops:
  6.5 82.8 %all-gather.13.cloned.1.call-start = ((), (), s32[]{:S(2)}) async-start(), calls=%async_computation | async-start | bytes 4718592 | tf_op jit(solution)/shard_map/all_gather | solution.py:12
  12.8 122.6 %all-gather.15.cloned.1.call-start = ((), (), s32[]{:S(2)}) async-start(), calls=%async_computation.1 | async-start | bytes 2621440 | tf_op jit(solution)/shard_map/all_gather | solution.py:12
  112.4 1.9 %copy-start.2 = (f32[4,128]{1,0:T(4,128)S(1)}, f32[4,128]{1,0:T(4,128)}, u32[]{:S(2)}) copy-start(f32[4,128]{1,0:T(4,128)} %param.14) | copy-start | bytes 6148
  112.4 2.2 %copy-start.1 = (bf16[128,512]{1,0:T(8,128)(2,1)S(1)}, bf16[128,512]{1,0:T(8,128)(2,1)}, u32[]{:S(2)}) copy-start(bf16[128,512]{1,0:T(8,128)(2,1)} %param.12) | copy-start | bytes 393220
  112.4 2.2 %copy-start.3 = (bf16[128,512]{1,0:T(8,128)(2,1)S(1)}, bf16[128,512]{1,0:T(8,128)(2,1)}, u32[]{:S(2)}) copy-start(bf16[128,512]{1,0:T(8,128)(2,1)} %param.11) | copy-start | bytes 393220
  135.3 10.6 %copy-start = (bf16[128,1024]{1,0:T(8,128)(2,1)S(1)}, bf16[128,1024]{1,0:T(8,128)(2,1)}, u32[]{:S(2)}) copy-start(bf16[128,1024]{1,0:T(8,128)(2,1)} %param.13) | copy-start | bytes 786436
Sparse Core Ops, SparseCore 0:
  12.9 76.4 all-gather.12
  114.3 20.9 all-gather.14
where the time goes:
time: 157 us; the launch traced here: 155 us
  blocking collectives  60.5 us (39%)
  waiting for transfers between devices  30.5 us (19%)
  other arithmetic  29.2 us (19%)
  between operations  14.8 us (9%)
  local copies, waits for them, and re-layouts  12.2 us (8%)
  matrix products  8.03 us (5%)
    all_gather x2, blocking collectives, prefix_2(): pieces = jax.tree.map(lambda part: lax.all_gather(part, axis), value)  31.5 us
    all_gather x2, waiting for transfers between devices, prefix_2(): pieces = jax.tree.map(lambda part: lax.all_gather(part, axis), value)  30.4 us
    unnamed x2, blocking collectives  29 us
    select_n x51, other arithmetic, lap(): jnp.where(position < mine, new, old)  22 us
    rev x4, local copies, waits for them, and re-layouts, prefix_2(): pieces = jax.tree.map(lambda part: part[::-1], pieces)  4.63 us
    dot_general x4, matrix products, on_device(): jnp.dot(query_widened, prev_vector[head_index], precision=exact_precision...  3.15 us
  transfers between devices with their start and end apart: 2, of which 2 were waited for; matrix products, arithmetic and copies ran while one was open for 4% of the time, Pallas kernels for 0%

commit v1 on v0

v1 whole, which is shorter than its diff:
```python
import functools

import jax
import jax.numpy as jnp
from jax import lax
from jax.experimental import pallas as pl
from jax.experimental.pallas import tpu as pltpu
from jax.sharding import PartitionSpec as P

floor_value = -1e30
LANES = 128
AXES = ("grp", "seq")


def split_two(x):
    high = x.astype(jnp.bfloat16)
    low = (x - high.astype(jnp.float32)).astype(jnp.bfloat16)
    return high, low


def split_three(x):
    high = x.astype(jnp.bfloat16)
    rest = x - high.astype(jnp.float32)
    mid = rest.astype(jnp.bfloat16)
    low = (rest - mid.astype(jnp.float32)).astype(jnp.bfloat16)
    return high, mid, low


def dot(a, b):
    return jnp.dot(a, b, preferred_element_type=jnp.float32)


def dot_last(a, b):
    return lax.dot_general(a, b, (((1,), (1,)), ((), ())), preferred_element_type=jnp.float32)


def log_forget(forget):
    return jnp.minimum(forget, 0.0) - jnp.log1p(jnp.exp(-jnp.abs(forget)))


def triangle(length, lower):
    rows = lax.broadcasted_iota(jnp.int32, (length, length), 0)
    cols = lax.broadcasted_iota(jnp.int32, (length, length), 1)
    return rows >= cols if lower else rows <= cols


def cumulative_rows(logf):
    ones = triangle(logf.shape[1], False).astype(jnp.bfloat16)
    high, mid, low = split_three(logf)
    return (dot(low, ones) + dot(mid, ones)) + dot(high, ones)


def cumulative_columns(logf):
    ones = triangle(logf.shape[1], True).astype(jnp.bfloat16)
    high, mid, low = split_three(logf)
    return (dot_last(ones, low) + dot_last(ones, mid)) + dot_last(ones, high)


def state_kernel(key_rows, k_ref, v_ref, in_ref, fo_ref, msg_ref):
    heads, length = in_ref.shape
    key_dim = k_ref.shape[1] // heads
    value_dim = v_ref.shape[1] // heads
    parts = value_dim // LANES
    per_head = key_dim // key_rows
    matrix_rows = parts * key_rows
    pad_rows = msg_ref.shape[1] - matrix_rows - 3
    cumul = cumulative_rows(log_forget(fo_ref[...]))
    level = in_ref[...] - cumul
    level_top = jnp.max(level, axis=1, keepdims=True)
    weight = jnp.exp(level - level_top)
    decay = cumul[:, length - 1 : length]
    top = decay + level_top
    for head in range(heads):
        keys = k_ref[:, head * key_dim : (head + 1) * key_dim]
        values = v_ref[:, head * value_dim : (head + 1) * value_dim]
        row = weight[head : head + 1, :]
        high, low = split_two(keys.astype(jnp.float32).T * row)
        matrix = dot(
            jnp.concatenate([high, low], axis=1), jnp.concatenate([values, values], axis=0)
        )
        high, mid, low = split_three(row)
        vector = (dot(low, keys) + dot(mid, keys)) + dot(high, keys)
        tail = [
            vector,
            jnp.broadcast_to(top[head : head + 1, :], (1, key_dim)),
            jnp.broadcast_to(decay[head : head + 1, :], (1, key_dim)),
        ]
        if pad_rows:
            tail.append(jnp.zeros((pad_rows, key_dim), jnp.float32))
        tail = jnp.concatenate(tail, axis=0)
        for piece in range(per_head):
            slot = head * per_head + piece
            for part in range(parts):
                msg_ref[slot, part * key_rows : (part + 1) * key_rows, :] = matrix[
                    piece * key_rows : (piece + 1) * key_rows, part * LANES : (part + 1) * LANES
                ]
            msg_ref[slot, matrix_rows:, :] = tail


def scan_kernel(matrix_rows, in_ref, out_ref):
    count, rows, lanes = in_ref.shape
    at_top = lax.broadcasted_iota(jnp.int32, (rows, lanes), 0) == matrix_rows + 1

    def step(block, carry):
        state, top = carry
        out_ref[block] = jnp.where(at_top, top, state)
        piece = in_ref[block]
        own_top = piece[matrix_rows + 1 : matrix_rows + 2, :]
        moved = top + piece[matrix_rows + 2 : matrix_rows + 3, :]
        joined = jnp.maximum(moved, own_top)
        state = jnp.exp(moved - joined) * state + jnp.exp(own_top - joined) * piece
        return state, joined

    carry = (
        jnp.zeros((rows, lanes), jnp.float32),
        jnp.full((1, lanes), floor_value, jnp.float32),
    )
    lax.fori_loop(0, count, step, carry, unroll=min(count, 32))


def inner_kernel(q_ref, k_ref, v_ref, in_ref, fo_ref, num_ref, stat_ref):
    heads, length = in_ref.shape
    key_dim = q_ref.shape[1] // heads
    value_dim = v_ref.shape[1] // heads
    logf = log_forget(fo_ref[...])
    level = in_ref[...] - cumulative_rows(logf)
    stat_ref[:, 0:heads] = cumulative_columns(logf)
    causal = triangle(length, True)
    for head in range(heads):
        queries = q_ref[:, head * key_dim : (head + 1) * key_dim]
        keys = k_ref[:, head * key_dim : (head + 1) * key_dim]
        values = v_ref[:, head * value_dim : (head + 1) * value_dim]
        scores = dot_last(queries, keys) * (key_dim**-0.5)
        masked = jnp.where(causal, level[head : head + 1, :], -jnp.inf)
        row_level = jnp.max(masked, axis=1, keepdims=True)
        weighted = jnp.exp(masked - row_level) * scores
        stat_ref[:, heads + head : heads + head + 1] = row_level
        stat_ref[:, 2 * heads + head : 2 * heads + head + 1] = jnp.sum(
            weighted, axis=1, keepdims=True
        )
        num_ref[:, head * value_dim : (head + 1) * value_dim] = dot(
            weighted.astype(jnp.bfloat16), values
        )


def outer_kernel(key_rows, q_ref, msg_ref, num_ref, stat_ref, out_ref, left_ref):
    count, rows, _ = msg_ref.shape
    heads = stat_ref.shape[1] // 3
    key_dim = q_ref.shape[1] // heads
    value_dim = num_ref.shape[1] // heads
    parts = value_dim // LANES
    per_head = key_dim // key_rows
    matrix_rows = parts * key_rows
    scaling = key_dim**-0.5
    for head in range(heads):
        first = head * per_head
        columns = []
        for part in range(parts):
            place = slice(part * key_rows, (part + 1) * key_rows)
            if key_rows % 8 == 0:
                columns.append(
                    msg_ref[first : first + per_head, place, :].reshape(key_dim, LANES)
                )
            else:
                for piece in range(per_head):
                    left_ref[piece * key_rows : (piece + 1) * key_rows, :] = msg_ref[
                        first + piece, place, :
                    ]
                columns.append(left_ref[...])
        high, low = split_two(jnp.concatenate(columns, axis=1))
        queries = q_ref[:, head * key_dim : (head + 1) * key_dim]
        carried = dot(
            jnp.concatenate([queries, queries], axis=1), jnp.concatenate([high, low], axis=0)
        )
        vector = msg_ref[first, matrix_rows : matrix_rows + 1, :]
        top = msg_ref[first, matrix_rows + 1 : matrix_rows + 2, 0:1]
        carried_den = jnp.sum(queries.astype(jnp.float32) * vector, axis=1, keepdims=True)
        cumul = stat_ref[:, head : head + 1]
        row_level = stat_ref[:, heads + head : heads + head + 1]
        inner_den = stat_ref[:, 2 * heads + head : 2 * heads + head + 1]
        joined = jnp.maximum(row_level, top)
        inner_factor = jnp.exp(row_level - joined)
        outer_factor = jnp.exp(top - joined) * scaling
        denom = inner_factor * inner_den + outer_factor * carried_den
        floor = jnp.exp(-(cumul + joined))
        inverse = 1.0 / jnp.maximum(jnp.abs(denom), floor)
        numer = (
            inner_factor * num_ref[:, head * value_dim : (head + 1) * value_dim]
            + outer_factor * carried
        )
        out_ref[:, head * value_dim : (head + 1) * value_dim] = (numer * inverse).astype(
            out_ref.dtype
        )


def on_device(device_count, queries, key_vectors, value_vectors, input_gate, forget_gate):
    heads, length = input_gate.shape
    key_dim = queries.shape[1] // heads
    value_dim = value_vectors.shape[1] // heads
    key_rows = heads * key_dim // device_count
    matrix_rows = (value_dim // LANES) * key_rows
    rows = -(-(matrix_rows + 3) // 8) * 8
    message = jax.ShapeDtypeStruct((device_count, rows, LANES), jnp.float32)
    params = pltpu.CompilerParams(vmem_limit_bytes=48 * 1024 * 1024)

    own = pl.pallas_call(
        functools.partial(state_kernel, key_rows), out_shape=message, compiler_params=params
    )(key_vectors, value_vectors, input_gate, forget_gate)
    gathered = lax.all_to_all(own, AXES, 0, 0)
    inner_num, stats = pl.pallas_call(
        inner_kernel,
        out_shape=(
            jax.ShapeDtypeStruct((length, heads * value_dim), jnp.float32),
            jax.ShapeDtypeStruct((length, 3 * heads), jnp.float32),
        ),
        compiler_params=params,
    )(queries, key_vectors, value_vectors, input_gate, forget_gate)
    before = pl.pallas_call(
        functools.partial(scan_kernel, matrix_rows), out_shape=message, compiler_params=params
    )(gathered)
    carried = lax.all_to_all(before, AXES, 0, 0)
    return pl.pallas_call(
        functools.partial(outer_kernel, key_rows),
        out_shape=jax.ShapeDtypeStruct((length, heads * value_dim), jnp.bfloat16),
        scratch_shapes=[pltpu.VMEM((key_dim, LANES), jnp.float32)],
        compiler_params=params,
    )(queries, carried, inner_num, stats)


def solution(mesh):
    device_count = mesh.shape["grp"] * mesh.shape["seq"]
    return jax.shard_map(
        functools.partial(on_device, device_count),
        mesh=mesh,
        in_specs=(
            P(AXES, None),
            P(AXES, None),
            P(AXES, None),
            P(None, AXES),
            P(None, AXES),
        ),
        out_specs=P(AXES, None),
        check_vma=False,
    )
```

time: 157 us -> 55.4 us (0.35)
  blocking collectives: 60.5 us -> 26.3 us
  other arithmetic: 29.2 us -> 0 us
  between operations: 14.8 us -> 0.07 us
  waiting for transfers between devices: 30.5 us -> 18.2 us
  local copies, waits for them, and re-layouts: 12.2 us -> 3.24 us
  matrix products: 8.03 us -> 0 us
  Pallas kernels: 0 us -> 4.55 us
  starting transfers between devices: 0.04 us -> 2.76 us
    all_gather x2 -> x0, blocking collectives: 31.5 us -> none  [prefix_2(): pieces = jax.tree.map(lambda part: lax.all_gather(part, axis), value)]
    all_gather x2 -> x0, waiting for transfers between devices: 30.4 us -> none  [prefix_2(): pieces = jax.tree.map(lambda part: lax.all_gather(part, axis), value)]
    unnamed x2 -> x0, blocking collectives: 29 us -> none
    all_to_all x0 -> x1, blocking collectives: none -> 26.3 us  [on_device(): gathered = lax.all_to_all(own, AXES, 0, 0)]
    select_n x51 -> x0, other arithmetic: 22 us -> none  [lap(): jnp.where(position < mine, new, old)]
    all_to_all x0 -> x1, waiting for transfers between devices: none -> 18.2 us  [on_device(): carried = lax.all_to_all(before, AXES, 0, 0)]
    dot_general x18 -> x0, matrix products: 8.03 us -> none  [the longest x4 3.15 us: on_device(): jnp.dot(query_widened, prev_vector[head_index], precision=exact_precision...]
    rev x4 -> x0, local copies, waits for them, and re-layouts: 4.63 us -> none  [prefix_2(): pieces = jax.tree.map(lambda part: part[::-1], pieces)]
  transfers between devices with their start and end apart: 2 -> 1, of which waited for: 2 -> 1; matrix products, arithmetic and copies ran while one was open for 4% -> 0% of each run, Pallas kernels for 0% -> 2%
where the time goes in v1:
time: 55.4 us; the launch traced here: 55.1 us
  blocking collectives  26.3 us (47%)
  waiting for transfers between devices  18.2 us (33%)
  Pallas kernels  4.55 us (8%)
  local copies, waits for them, and re-layouts  3.24 us (6%)
  starting transfers between devices  2.76 us (5%)
    all_to_all x1, blocking collectives, on_device(): gathered = lax.all_to_all(own, AXES, 0, 0)  26.3 us
    all_to_all x1, waiting for transfers between devices, on_device(): carried = lax.all_to_all(before, AXES, 0, 0)  18.2 us
    unnamed x18, local copies, waits for them, and re-layouts  3.24 us
    all_to_all x1, starting transfers between devices, on_device(): carried = lax.all_to_all(before, AXES, 0, 0)  2.76 us
    pallas_call x1, Pallas kernels, on_device(): pl.pallas_call(functools.partial(outer_kernel, key_rows), out_shape=jax.S...  2.16 us
  transfers between devices with their start and end apart: 1, of which 1 were waited for; matrix products, arithmetic and copies ran while one was open for 0% of the time, Pallas kernels for 2%

profile of v1, /device:TPU:0, one launch (start us, length us, event | category | flops | bytes accessed | tf_op | source)
XLA Modules:
  0.0 55.1 jit_solution(18392869801498002496)
XLA Ops:
  0.0 0.0 copy-start
  0.0 0.9 %copy-done = bf16[128,1024]{1,0:T(8,128)(2,1)S(1)} copy-done((bf16[128,1024]{1,0:T(8,128)(2,1)S(1)}, bf16[128,1024]{1,0:T(8,128)(2,1)}, u32[]{:S(2)}) %copy-start) | copy-done | bytes 262168
  1.0 0.0 copy-start.3
  1.0 0.9 %copy-done.3 = bf16[128,512]{1,0:T(8,128)(2,1)S(1)} copy-done((bf16[128,512]{1,0:T(8,128)(2,1)S(1)}, bf16[128,512]{1,0:T(8,128)(2,1)}, u32[]{:S(2)}) %copy-start.3) | copy-done | bytes 131096
  1.9 0.0 copy-start.5
  1.9 0.7 %copy-done.5 = f32[4,128]{1,0:T(4,128)S(1)} copy-done((f32[4,128]{1,0:T(4,128)S(1)}, f32[4,128]{1,0:T(4,128)}, u32[]{:S(2)}) %copy-start.5) | copy-done | bytes 2072
  2.5 0.0 copy-start.7
  2.5 0.7 %copy-done.7 = f32[4,128]{1,0:T(4,128)S(1)} copy-done((f32[4,128]{1,0:T(4,128)S(1)}, f32[4,128]{1,0:T(4,128)}, u32[]{:S(2)}) %copy-start.7) | copy-done | bytes 2072
  3.2 0.5 shard_map.55
  3.8 26.3 %all_to_all.10.in_ref = f32[32,40,128]{2,1,0:T(8,128)S(1)} all-to-all(f32[32,40,128]{2,1,0:T(8,128)S(1)} %shard_map.55), channel_id=1, replica_groups=mesh['grp'=4,'seq'=8] {'grp','seq'}, dimensions={0} | all-to-all | bytes 1310720 | tf_op jit(solution)/shard_map/all_to_all | solution.py:209
  30.0 1.0 %shard_map.56 = f32[32,40,128]{2,1,0:T(8,128)} custom-call(f32[32,40,128]{2,1,0:T(8,128)S(1)} %all_to_all.10.in_ref), custom_call_target="tpu_custom_call" | custom-call | tf_op jit(solution)/shard_map/pallas_call | solution.py:218
  31.0 0.0 copy-start.1
  31.0 0.0 copy-start.2
  31.0 0.0 copy-start.4
  31.0 0.0 copy-start.6
  31.0 0.0 copy-start.8
  31.0 2.8 %all-to-all-start.1 = ((f32[32,40,128]{2,1,0:T(8,128)}), f32[32,40,128]{2,1,0:T(8,128)S(1)}, u32[]{:S(2)}, u32[]{:S(2)}) async-start(f32[32,40,128]{2,1,0:T(8,128)} %shard_map.56), calls=%async_computation.1 | async-start | bytes 1310720 | tf_op jit(solution)/shard_map/all_to_all | solution.py:221
  33.8 0.0 copy-done.1
  33.8 0.0 copy-done.2
  33.8 0.0 copy-done.4
  33.8 0.0 copy-done.6
  33.8 0.0 copy-done.8
  33.8 0.9 %shard_map.57 = (f32[128,1024]{1,0:T(8,128)S(1)}, f32[128,12]{1,0:T(8,128)S(1)}) custom-call(bf16[128,512]{1,0:T(8,128)(2,1)S(1)} %copy-done.2, bf16[128,512]{1,0:T(8,128)(2,1)S(1)} %copy-done.4, bf16[128,1024]{1,0:T(8,128)(2,1)S(1)} %copy-done.1, f32[4,128]{1,0:T(4,128)S(1)} %copy-done.6, f32[4,128]{1,0:T(4,128)S(1)} %copy-done.8), custom_call_target="tpu_custom_call" | custom-call | tf_op jit(solution)/shard_map/pallas_call | solution.py:210
  34.7 18.2 %all-to-all-done.1.msg_ref = f32[32,40,128]{2,1,0:T(8,128)S(1)} async-done(((f32[32,40,128]{2,1,0:T(8,128)}), f32[32,40,128]{2,1,0:T(8,128)S(1)}, u32[]{:S(2)}, u32[]{:S(2)}) %all-to-all-start.1) | async-done | bytes 655392 | tf_op jit(solution)/shard_map/all_to_all | solution.py:221
  53.0 2.2 %shard_map.58 = bf16[128,1024]{1,0:T(8,128)(2,1)} custom-call(bf16[128,512]{1,0:T(8,128)(2,1)S(1)} %copy-done.2, f32[32,40,128]{2,1,0:T(8,128)S(1)} %all-to-all-done.1.msg_ref, f32[128,1024]{1,0:T(8,128)S(1)} %get-tuple-element.7.num_ref, f32[128,12]{1,0:T(8,128)S(1)} %get-tuple-element.8.stat_ref), custom_call_target="tpu_custom_call" | custom-call | tf_op jit(solution)/shard_map/pallas_call | solution.py:222
Async XLA Ops:
  0.0 0.9 %copy-start = (bf16[128,1024]{1,0:T(8,128)(2,1)S(1)}, bf16[128,1024]{1,0:T(8,128)(2,1)}, u32[]{:S(2)}) copy-start(bf16[128,1024]{1,0:T(8,128)(2,1)} %v_ref.3) | copy-start | bytes 786436
  1.0 0.9 %copy-start.3 = (bf16[128,512]{1,0:T(8,128)(2,1)S(1)}, bf16[128,512]{1,0:T(8,128)(2,1)}, u32[]{:S(2)}) copy-start(bf16[128,512]{1,0:T(8,128)(2,1)} %k_ref.3) | copy-start | bytes 393220
  1.9 0.7 %copy-start.5 = (f32[4,128]{1,0:T(4,128)S(1)}, f32[4,128]{1,0:T(4,128)}, u32[]{:S(2)}) copy-start(f32[4,128]{1,0:T(4,128)} %in_ref.3) | copy-start | bytes 6148
  2.5 0.7 %copy-start.7 = (f32[4,128]{1,0:T(4,128)S(1)}, f32[4,128]{1,0:T(4,128)}, u32[]{:S(2)}) copy-start(f32[4,128]{1,0:T(4,128)} %fo_ref.3) | copy-start | bytes 6148
  31.0 2.8 %copy-start.1 = (bf16[128,1024]{1,0:T(8,128)(2,1)S(1)}, bf16[128,1024]{1,0:T(8,128)(2,1)}, u32[]{:S(2)}) copy-start(bf16[128,1024]{1,0:T(8,128)(2,1)} %v_ref.3) | copy-start | bytes 786436
  31.0 2.8 %copy-start.2 = (bf16[128,512]{1,0:T(8,128)(2,1)S(1)}, bf16[128,512]{1,0:T(8,128)(2,1)}, u32[]{:S(2)}) copy-start(bf16[128,512]{1,0:T(8,128)(2,1)} %q_ref.3) | copy-start | bytes 393220
  31.0 2.8 %copy-start.4 = (bf16[128,512]{1,0:T(8,128)(2,1)S(1)}, bf16[128,512]{1,0:T(8,128)(2,1)}, u32[]{:S(2)}) copy-start(bf16[128,512]{1,0:T(8,128)(2,1)} %k_ref.3) | copy-start | bytes 393220
  31.0 2.8 %copy-start.6 = (f32[4,128]{1,0:T(4,128)S(1)}, f32[4,128]{1,0:T(4,128)}, u32[]{:S(2)}) copy-start(f32[4,128]{1,0:T(4,128)} %in_ref.3) | copy-start | bytes 6148
  31.0 2.8 %copy-start.8 = (f32[4,128]{1,0:T(4,128)S(1)}, f32[4,128]{1,0:T(4,128)}, u32[]{:S(2)}) copy-start(f32[4,128]{1,0:T(4,128)} %fo_ref.3) | copy-start | bytes 6148
  31.0 21.9 %all-to-all-start.1 = ((f32[32,40,128]{2,1,0:T(8,128)}), f32[32,40,128]{2,1,0:T(8,128)S(1)}, u32[]{:S(2)}, u32[]{:S(2)}) async-start(f32[32,40,128]{2,1,0:T(8,128)} %shard_map.56), calls=%async_computation.1 | async-start | bytes 1310720 | tf_op jit(solution)/shard_map/all_to_all | solution.py:221

commit v2 on v1

v2 whole, which is shorter than its diff:
```python
import functools

import jax
import jax.numpy as jnp
from jax import lax
from jax.experimental import pallas as pl
from jax.experimental.pallas import tpu as pltpu
from jax.sharding import PartitionSpec as P

floor_value = -1e30
LANES = 128
AXES = ("grp", "seq")


def split_two(x):
    high = x.astype(jnp.bfloat16)
    low = (x - high.astype(jnp.float32)).astype(jnp.bfloat16)
    return high, low


def split_three(x):
    high = x.astype(jnp.bfloat16)
    rest = x - high.astype(jnp.float32)
    mid = rest.astype(jnp.bfloat16)
    low = (rest - mid.astype(jnp.float32)).astype(jnp.bfloat16)
    return high, mid, low


def dot(a, b):
    return jnp.dot(a, b, preferred_element_type=jnp.float32)


def dot_last(a, b):
    return lax.dot_general(a, b, (((1,), (1,)), ((), ())), preferred_element_type=jnp.float32)


def log_forget(forget):
    return jnp.minimum(forget, 0.0) - jnp.log1p(jnp.exp(-jnp.abs(forget)))


def triangle(length, lower):
    rows = lax.broadcasted_iota(jnp.int32, (length, length), 0)
    cols = lax.broadcasted_iota(jnp.int32, (length, length), 1)
    return rows >= cols if lower else rows <= cols


def cumulative_rows(logf):
    ones = triangle(logf.shape[1], False).astype(jnp.bfloat16)
    high, mid, low = split_three(logf)
    return (dot(low, ones) + dot(mid, ones)) + dot(high, ones)


def cumulative_columns(logf):
    ones = triangle(logf.shape[1], True).astype(jnp.bfloat16)
    high, mid, low = split_three(logf)
    return (dot_last(ones, low) + dot_last(ones, mid)) + dot_last(ones, high)


def message_rows(matrix_rows):
    return matrix_rows + 2


def state_kernel(
    key_rows, k_hbm, v_hbm, in_hbm, fo_hbm, msg_ref, k_ref, v_ref, in_ref, fo_ref, arrived
):
    copies = [
        pltpu.make_async_copy(source, target, arrived.at[place])
        for place, (source, target) in enumerate(
            ((fo_hbm, fo_ref), (in_hbm, in_ref), (k_hbm, k_ref), (v_hbm, v_ref))
        )
    ]
    for copy in copies:
        copy.start()
    heads, length = in_ref.shape
    key_dim = k_ref.shape[1] // heads
    value_dim = v_ref.shape[1] // heads
    parts = value_dim // LANES
    per_head = key_dim // key_rows
    matrix_rows = parts * key_rows
    left = lax.broadcasted_iota(jnp.int32, (1, LANES), 1) < LANES // 2
    copies[0].wait()
    cumul = cumulative_rows(log_forget(fo_ref[...]))
    copies[1].wait()
    level = in_ref[...] - cumul
    level_top = jnp.max(level, axis=1, keepdims=True)
    weight = jnp.exp(level - level_top)
    decay = cumul[:, length - 1 : length]
    top = decay + level_top
    copies[2].wait()
    copies[3].wait()
    for head in range(heads):
        keys = k_ref[:, head * key_dim : (head + 1) * key_dim]
        values = v_ref[:, head * value_dim : (head + 1) * value_dim]
        row = weight[head : head + 1, :]
        high, low = split_two(keys.astype(jnp.float32).T * row)
        matrix = dot(
            jnp.concatenate([high, low], axis=1), jnp.concatenate([values, values], axis=0)
        )
        high, mid, low = split_three(row)
        vector = (dot(low, keys) + dot(mid, keys)) + dot(high, keys)
        scalars = jnp.where(left, top[head : head + 1, :], decay[head : head + 1, :])
        for piece in range(per_head):
            slot = head * per_head + piece
            for part in range(parts):
                msg_ref[slot, part * key_rows : (part + 1) * key_rows, 0, :] = matrix[
                    piece * key_rows : (piece + 1) * key_rows, part * LANES : (part + 1) * LANES
                ]
            msg_ref[slot, matrix_rows : matrix_rows + 1, 0, :] = vector
            msg_ref[slot, matrix_rows + 1 : matrix_rows + 2, 0, :] = scalars


def scan_kernel(in_ref, out_ref):
    count, rows, _, lanes = in_ref.shape
    left = lax.broadcasted_iota(jnp.int32, (1, lanes), 1) < lanes // 2

    def step(block, carry):
        state, top = carry
        out_ref[block, 0 : rows - 1, 0, :] = state
        out_ref[block, rows - 1 : rows, 0, :] = top
        piece = in_ref[block, 0 : rows - 1, 0, :]
        own = in_ref[block, rows - 1 : rows, 0, :]
        swapped = pltpu.roll(own, lanes // 2, 1)
        own_top = jnp.where(left, own, swapped)
        moved = top + jnp.where(left, swapped, own)
        joined = jnp.maximum(moved, own_top)
        state = jnp.exp(moved - joined) * state + jnp.exp(own_top - joined) * piece
        return state, joined

    carry = (
        jnp.zeros((rows - 1, lanes), jnp.float32),
        jnp.full((1, lanes), floor_value, jnp.float32),
    )
    lax.fori_loop(0, count, step, carry, unroll=min(count, 32))


def inner_kernel(q_ref, k_ref, v_ref, in_ref, fo_ref, num_ref, stat_ref):
    heads, length = in_ref.shape
    key_dim = q_ref.shape[1] // heads
    value_dim = v_ref.shape[1] // heads
    logf = log_forget(fo_ref[...])
    level = in_ref[...] - cumulative_rows(logf)
    stat_ref[:, 0:heads] = cumulative_columns(logf)
    causal = triangle(length, True)
    for head in range(heads):
        queries = q_ref[:, head * key_dim : (head + 1) * key_dim]
        keys = k_ref[:, head * key_dim : (head + 1) * key_dim]
        values = v_ref[:, head * value_dim : (head + 1) * value_dim]
        scores = dot_last(queries, keys) * (key_dim**-0.5)
        masked = jnp.where(causal, level[head : head + 1, :], -jnp.inf)
        row_level = jnp.max(masked, axis=1, keepdims=True)
        weighted = jnp.exp(masked - row_level) * scores
        stat_ref[:, heads + head : heads + head + 1] = row_level
        stat_ref[:, 2 * heads + head : 2 * heads + head + 1] = jnp.sum(
            weighted, axis=1, keepdims=True
        )
        num_ref[:, head * value_dim : (head + 1) * value_dim] = dot(
            weighted.astype(jnp.bfloat16), values
        )


def outer_kernel(
    key_rows, q_ref, msg_ref, num_ref, stat_ref, out_hbm, piece_ref, out_ref, done
):
    heads = stat_ref.shape[1] // 3
    key_dim = q_ref.shape[1] // heads
    value_dim = num_ref.shape[1] // heads
    parts = value_dim // LANES
    per_head = key_dim // key_rows
    matrix_rows = parts * key_rows
    scaling = key_dim**-0.5

    head_of = lax.broadcasted_iota(jnp.int32, (1, heads), 1)
    top = jnp.zeros((1, heads), jnp.float32)
    vectors = []
    for head in range(heads):
        first = head * per_head
        own_top = msg_ref[first, matrix_rows + 1 : matrix_rows + 2, 0, :]
        top = jnp.where(head_of == head, own_top[:, 0:1], top)
        vector = msg_ref[first, matrix_rows : matrix_rows + 1, 0, :]
        zero = jnp.zeros_like(vector)
        vectors.append(jnp.concatenate([zero] * head + [vector] + [zero] * (heads - 1 - head), 1))
    terms = split_three(jnp.concatenate(vectors, axis=0))
    queries = q_ref[...]
    carried_den = dot_last(queries, terms[2]) + dot_last(queries, terms[1])
    carried_den = (carried_den + dot_last(queries, terms[0])) * scaling
    cumul = stat_ref[:, 0:heads]
    row_level = stat_ref[:, heads : 2 * heads]
    inner_den = stat_ref[:, 2 * heads : 3 * heads]
    joined = jnp.maximum(row_level, top)
    inner_factor = jnp.exp(row_level - joined)
    outer_factor = jnp.exp(top - joined)
    denom = inner_factor * inner_den + outer_factor * carried_den
    inverse = 1.0 / jnp.maximum(jnp.abs(denom), jnp.exp(-(cumul + joined)))
    inner_factor = inner_factor * inverse
    outer_factor = outer_factor * (inverse * scaling)

    copies = []
    for head in range(heads):
        first = head * per_head
        columns = []
        for part in range(parts):
            place = slice(part * key_rows, (part + 1) * key_rows)
            if key_rows % 8 == 0:
                columns.append(
                    msg_ref[first : first + per_head, place, 0, :].reshape(key_dim, LANES)
                )
            else:
                for piece in range(per_head):
                    piece_ref[piece * key_rows : (piece + 1) * key_rows, :] = msg_ref[
                        first + piece, place, 0, :
                    ]
                columns.append(piece_ref[...])
        high, low = split_two(jnp.concatenate(columns, axis=1))
        query = queries[:, head * key_dim : (head + 1) * key_dim]
        carried = dot(
            jnp.concatenate([query, query], axis=1), jnp.concatenate([high, low], axis=0)
        )
        place = pl.ds(head * value_dim, value_dim)
        out_ref[:, place] = (
            inner_factor[:, head : head + 1] * num_ref[:, place]
            + outer_factor[:, head : head + 1] * carried
        ).astype(out_ref.dtype)
        copy = pltpu.make_async_copy(out_ref.at[:, place], out_hbm.at[:, place], done.at[head])
        copy.start()
        copies.append(copy)
    for copy in copies:
        copy.wait()


def on_device(device_count, queries, key_vectors, value_vectors, input_gate, forget_gate):
    heads, length = input_gate.shape
    key_dim = queries.shape[1] // heads
    value_dim = value_vectors.shape[1] // heads
    key_rows = heads * key_dim // device_count
    matrix_rows = (value_dim // LANES) * key_rows
    message = jax.ShapeDtypeStruct(
        (device_count, message_rows(matrix_rows), 1, LANES), jnp.float32
    )
    params = pltpu.CompilerParams(vmem_limit_bytes=48 * 1024 * 1024)
    hbm = pl.BlockSpec(memory_space=pltpu.HBM)
    output = jax.ShapeDtypeStruct((length, heads * value_dim), jnp.bfloat16)
    operands = (key_vectors, value_vectors, input_gate, forget_gate)

    own = pl.pallas_call(
        functools.partial(state_kernel, key_rows),
        out_shape=message,
        in_specs=[hbm] * len(operands),
        scratch_shapes=[pltpu.VMEM(array.shape, array.dtype) for array in operands]
        + [pltpu.SemaphoreType.DMA((len(operands),))],
        compiler_params=params,
    )(*(pltpu.with_memory_space_constraint(array, pltpu.HBM) for array in operands))
    gathered = lax.all_to_all(own, AXES, 0, 0)
    inner_num, stats = pl.pallas_call(
        inner_kernel,
        out_shape=(
            jax.ShapeDtypeStruct((length, heads * value_dim), jnp.float32),
            jax.ShapeDtypeStruct((length, 3 * heads), jnp.float32),
        ),
        compiler_params=params,
    )(queries, *operands)
    before = pl.pallas_call(scan_kernel, out_shape=message, compiler_params=params)(gathered)
    carried = lax.all_to_all(before, AXES, 0, 0)
    return pl.pallas_call(
        functools.partial(outer_kernel, key_rows),
        out_shape=output,
        out_specs=hbm,
        scratch_shapes=[
            pltpu.VMEM((key_dim, LANES), jnp.float32),
            pltpu.VMEM(output.shape, output.dtype),
            pltpu.SemaphoreType.DMA((heads,)),
        ],
        compiler_params=params,
    )(queries, carried, inner_num, stats)


def solution(mesh):
    device_count = mesh.shape["grp"] * mesh.shape["seq"]
    return jax.shard_map(
        functools.partial(on_device, device_count),
        mesh=mesh,
        in_specs=(
            P(AXES, None),
            P(AXES, None),
            P(AXES, None),
            P(None, AXES),
            P(None, AXES),
        ),
        out_specs=P(AXES, None),
        check_vma=False,
    )
```

time: 55.4 us -> 48.8 us (0.88)
  local copies, waits for them, and re-layouts: 3.24 us -> 0.02 us
  blocking collectives: 26.3 us -> 24.2 us
  waiting for transfers between devices: 18.2 us -> 16.1 us
  Pallas kernels: 4.55 us -> 5.41 us
    unnamed x18 -> x10, local copies, waits for them, and re-layouts: 3.24 us -> 0.02 us
    all_to_all x1, waiting for transfers between devices: 18.2 us -> 16.1 us  [on_device(): carried = lax.all_to_all(before, AXES, 0, 0)]
    all_to_all x1, blocking collectives: 26.3 us -> 24.2 us  [on_device(): gathered = lax.all_to_all(own, AXES, 0, 0)]
    pallas_call x1, Pallas kernels: 0.54 us -> 1.61 us  [on_device(): pl.pallas_call(functools.partial(state_kernel, key_rows), out_shape=messa...]
where the time goes in v2:
time: 48.8 us; the launch traced here: 48.5 us
  blocking collectives  24.2 us (50%)
  waiting for transfers between devices  16.1 us (33%)
  Pallas kernels  5.41 us (11%)
  starting transfers between devices  2.76 us (6%)
    all_to_all x1, blocking collectives, on_device(): gathered = lax.all_to_all(own, AXES, 0, 0)  24.2 us
    all_to_all x1, waiting for transfers between devices, on_device(): carried = lax.all_to_all(before, AXES, 0, 0)  16.1 us
    all_to_all x1, starting transfers between devices, on_device(): carried = lax.all_to_all(before, AXES, 0, 0)  2.76 us
    pallas_call x1, Pallas kernels, on_device(): pl.pallas_call(functools.partial(state_kernel, key_rows), out_shape=messa...  1.61 us
    pallas_call x1, Pallas kernels, on_device(): pl.pallas_call(scan_kernel, out_shape=message, compiler_params=params)  1.46 us
    pallas_call x1, Pallas kernels, on_device(): pl.pallas_call(functools.partial(outer_kernel, key_rows), out_shape=outpu...  1.46 us
  transfers between devices with their start and end apart: 1, of which 1 were waited for; matrix products, arithmetic and copies ran while one was open for 0% of the time, Pallas kernels for 2%

profile of v2, /device:TPU:0, one launch (start us, length us, event | category | flops | bytes accessed | tf_op | source)
XLA Modules:
  0.0 48.5 jit_solution(11803259675559612655)
XLA Ops:
  0.0 1.6 %shard_map.55 = f32[32,34,1,128]{3,2,1,0:T(1,128)S(1)} custom-call(bf16[128,512]{1,0:T(8,128)(2,1)} %k_ref.1, bf16[128,1024]{1,0:T(8,128)(2,1)} %v_ref.1, f32[4,128]{1,0:T(4,128)} %in_ref.1, f32[4,128]{1,0:T(4,128)} %fo_ref.1), custom_call_target="tpu_custom_call" | custom-call | tf_op jit(solution)/shard_map/pallas_call | solution.py:244
  1.6 24.2 %all_to_all.10.in_ref = f32[32,34,1,128]{3,2,1,0:T(1,128)S(1)} all-to-all(f32[32,34,1,128]{3,2,1,0:T(1,128)S(1)} %shard_map.55), channel_id=1, replica_groups=mesh['grp'=4,'seq'=8] {'grp','seq'}, dimensions={0} | all-to-all | bytes 1114112 | tf_op jit(solution)/shard_map/all_to_all | solution.py:252
  25.8 1.5 %shard_map.56 = f32[32,34,1,128]{3,2,1,0:T(1,128)} custom-call(f32[32,34,1,128]{3,2,1,0:T(1,128)S(1)} %all_to_all.10.in_ref), custom_call_target="tpu_custom_call" | custom-call | tf_op jit(solution)/shard_map/pallas_call | solution.py:261
  27.2 0.0 copy-start
  27.2 0.0 copy-start.1
  27.2 0.0 copy-start.2
  27.2 0.0 copy-start.3
  27.3 0.0 copy-start.4
  27.3 2.8 %all-to-all-start.1 = ((f32[32,34,1,128]{3,2,1,0:T(1,128)}), f32[32,34,1,128]{3,2,1,0:T(1,128)S(1)}, u32[]{:S(2)}, u32[]{:S(2)}) async-start(f32[32,34,1,128]{3,2,1,0:T(1,128)} %shard_map.56), calls=%async_computation.1 | async-start | bytes 1114112 | tf_op jit(solution)/shard_map/all_to_all | solution.py:262
  30.0 0.0 copy-done
  30.0 0.0 copy-done.1
  30.0 0.0 copy-done.2
  30.1 0.0 copy-done.3
  30.1 0.0 copy-done.4
  30.1 0.9 %shard_map.57 = (f32[128,1024]{1,0:T(8,128)S(1)}, f32[128,12]{1,0:T(8,128)S(1)}) custom-call(bf16[128,512]{1,0:T(8,128)(2,1)S(1)} %copy-done.1, bf16[128,512]{1,0:T(8,128)(2,1)S(1)} %copy-done.2, bf16[128,1024]{1,0:T(8,128)(2,1)S(1)} %copy-done, f32[4,128]{1,0:T(4,128)S(1)} %copy-done.3, f32[4,128]{1,0:T(4,128)S(1)} %copy-done.4), custom_call_target="tpu_custom_call" | custom-call | tf_op jit(solution)/shard_map/pallas_call | solution.py:253
  31.0 16.1 %all-to-all-done.1.msg_ref = f32[32,34,1,128]{3,2,1,0:T(1,128)S(1)} async-done(((f32[32,34,1,128]{3,2,1,0:T(1,128)}), f32[32,34,1,128]{3,2,1,0:T(1,128)S(1)}, u32[]{:S(2)}, u32[]{:S(2)}) %all-to-all-start.1) | async-done | bytes 557088 | tf_op jit(solution)/shard_map/all_to_all | solution.py:262
  47.1 1.5 %shard_map.58 = bf16[128,1024]{1,0:T(8,128)(2,1)} custom-call(bf16[128,512]{1,0:T(8,128)(2,1)S(1)} %copy-done.1, f32[32,34,1,128]{3,2,1,0:T(1,128)S(1)} %all-to-all-done.1.msg_ref, f32[128,1024]{1,0:T(8,128)S(1)} %get-tuple-element.7.num_ref, f32[128,12]{1,0:T(8,128)S(1)} %get-tuple-element.8.stat_ref), custom_call_target="tpu_custom_call" | custom-call | tf_op jit(solution)/shard_map/pallas_call | solution.py:263
Async XLA Ops:
  27.2 2.8 %copy-start = (bf16[128,1024]{1,0:T(8,128)(2,1)S(1)}, bf16[128,1024]{1,0:T(8,128)(2,1)}, u32[]{:S(2)}) copy-start(bf16[128,1024]{1,0:T(8,128)(2,1)} %v_ref.1) | copy-start | bytes 786436
  27.2 2.8 %copy-start.1 = (bf16[128,512]{1,0:T(8,128)(2,1)S(1)}, bf16[128,512]{1,0:T(8,128)(2,1)}, u32[]{:S(2)}) copy-start(bf16[128,512]{1,0:T(8,128)(2,1)} %q_ref.3) | copy-start | bytes 393220
  27.2 2.8 %copy-start.2 = (bf16[128,512]{1,0:T(8,128)(2,1)S(1)}, bf16[128,512]{1,0:T(8,128)(2,1)}, u32[]{:S(2)}) copy-start(bf16[128,512]{1,0:T(8,128)(2,1)} %k_ref.1) | copy-start | bytes 393220
  27.2 2.8 %copy-start.3 = (f32[4,128]{1,0:T(4,128)S(1)}, f32[4,128]{1,0:T(4,128)}, u32[]{:S(2)}) copy-start(f32[4,128]{1,0:T(4,128)} %in_ref.1) | copy-start | bytes 6148
  27.3 2.8 %copy-start.4 = (f32[4,128]{1,0:T(4,128)S(1)}, f32[4,128]{1,0:T(4,128)}, u32[]{:S(2)}) copy-start(f32[4,128]{1,0:T(4,128)} %fo_ref.1) | copy-start | bytes 6148
  27.3 19.8 %all-to-all-start.1 = ((f32[32,34,1,128]{3,2,1,0:T(1,128)}), f32[32,34,1,128]{3,2,1,0:T(1,128)S(1)}, u32[]{:S(2)}, u32[]{:S(2)}) async-start(f32[32,34,1,128]{3,2,1,0:T(1,128)} %shard_map.56), calls=%async_computation.1 | async-start | bytes 1114112 | tf_op jit(solution)/shard_map/all_to_all | solution.py:262

commit v3 on v2

v3 whole, which is shorter than its diff:
```python
import functools

import jax
import jax.numpy as jnp
from jax import lax
from jax.experimental import pallas as pl
from jax.experimental.pallas import tpu as pltpu
from jax.sharding import PartitionSpec as P

floor_value = -1e30
LANES = 128
AXES = ("grp", "seq")


def split_two(x):
    high = x.astype(jnp.bfloat16)
    low = (x - high.astype(jnp.float32)).astype(jnp.bfloat16)
    return high, low


def split_three(x):
    high = x.astype(jnp.bfloat16)
    rest = x - high.astype(jnp.float32)
    mid = rest.astype(jnp.bfloat16)
    low = (rest - mid.astype(jnp.float32)).astype(jnp.bfloat16)
    return high, mid, low


def dot(a, b):
    return jnp.dot(a, b, preferred_element_type=jnp.float32)


def dot_last(a, b):
    return lax.dot_general(a, b, (((1,), (1,)), ((), ())), preferred_element_type=jnp.float32)


def log_forget(forget):
    return jnp.minimum(forget, 0.0) - jnp.log1p(jnp.exp(-jnp.abs(forget)))


def triangle(length, lower):
    rows = lax.broadcasted_iota(jnp.int32, (length, length), 0)
    cols = lax.broadcasted_iota(jnp.int32, (length, length), 1)
    return rows >= cols if lower else rows <= cols


def cumulative_rows(logf):
    ones = triangle(logf.shape[1], False).astype(jnp.bfloat16)
    high, mid, low = split_three(logf)
    return (dot(low, ones) + dot(mid, ones)) + dot(high, ones)


def cumulative_columns(logf):
    ones = triangle(logf.shape[1], True).astype(jnp.bfloat16)
    high, mid, low = split_three(logf)
    return (dot_last(ones, low) + dot_last(ones, mid)) + dot_last(ones, high)


SIDES = 2
TAIL = 8
VECTOR, TOP, DECAY = range(3)


def member(quad):
    return lax.rem(lax.axis_index(AXES[1]), quad)


def own_side():
    return lax.rem(lax.axis_index(AXES[0]), SIDES)


def tail_row(ref, row, slot=0):
    return ref[pl.ds(ref.shape[0] - TAIL + 3 * slot + row, 1), :]


def load(ref, slot=0, slots=1):
    key_dim = (ref.shape[0] - TAIL) // slots
    rows = [tail_row(ref, row, slot) for row in range(3)]
    return (ref[slot * key_dim : (slot + 1) * key_dim, :], *rows)


def store(ref, *states):
    key_dim = states[0][0].shape[0]
    rows = []
    for slot, (matrix, *tail) in enumerate(states):
        ref[slot * key_dim : (slot + 1) * key_dim, :] = matrix
        rows += tail
    rows.append(jnp.zeros((TAIL - len(rows), ref.shape[1]), jnp.float32))
    ref[len(states) * key_dim :, :] = jnp.concatenate(rows, axis=0)


def join(earlier, later):
    early_matrix, early_vector, early_top, early_decay = earlier
    late_matrix, late_vector, late_top, late_decay = later
    moved = early_top + late_decay
    joined = jnp.maximum(moved, late_top)
    early_weight, late_weight = jnp.exp(moved - joined), jnp.exp(late_top - joined)
    return (
        early_weight * early_matrix + late_weight * late_matrix,
        early_weight * early_vector + late_weight * late_vector,
        joined,
        early_decay + late_decay,
    )


def choose(condition, one, other):
    return jax.tree.map(lambda a, b: jnp.where(condition, a, b), one, other)


def nothing(like):
    matrix, vector, top, decay = like
    zero = jnp.zeros_like(decay)
    return jnp.zeros_like(matrix), jnp.zeros_like(vector), zero + floor_value, zero


def state_kernel(k_hbm, v_hbm, in_hbm, fo_hbm, *refs):
    own_ref, send_ref, k_ref, v_ref, in_ref, fo_ref, arrived = refs
    copies = [
        pltpu.make_async_copy(source, target, arrived.at[place])
        for place, (source, target) in enumerate(
            ((fo_hbm, fo_ref), (in_hbm, in_ref), (k_hbm, k_ref), (v_hbm, v_ref))
        )
    ]
    for copy in copies:
        copy.start()
    heads, length = in_ref.shape
    key_dim = k_ref.shape[1] // heads
    value_dim = v_ref.shape[1] // heads
    copies[0].wait()
    cumul = cumulative_rows(log_forget(fo_ref[...]))
    copies[1].wait()
    level = in_ref[...] - cumul
    level_top = jnp.max(level, axis=1, keepdims=True)
    decay = cumul[:, length - 1 : length]
    weight = jnp.exp(level - level_top)
    top = decay + level_top
    first = own_side() == 0
    copies[2].wait()
    copies[3].wait()
    for head in range(heads):
        keys = k_ref[:, head * key_dim : (head + 1) * key_dim]
        values = v_ref[:, head * value_dim : (head + 1) * value_dim]
        row = weight[head : head + 1, :]
        high, low = split_two(keys.astype(jnp.float32).T * row)
        matrix = dot(
            jnp.concatenate([high, low], axis=1), jnp.concatenate([values, values], axis=0)
        )
        high, mid, low = split_three(row)
        vector = (dot(low, keys) + dot(mid, keys)) + dot(high, keys)
        tail = (
            vector,
            jnp.broadcast_to(top[head : head + 1, :], vector.shape),
            jnp.broadcast_to(decay[head : head + 1, :], vector.shape),
        )
        left, right = matrix[:, :LANES], matrix[:, LANES:]
        store(own_ref.at[head], (jnp.where(first, left, right), *tail))
        store(send_ref.at[head], (jnp.where(first, right, left), *tail))


def pack_kernel(own_ref, other_ref, *out_refs):
    me, first = member(len(out_refs)), own_side() == 0
    for step, out_ref in enumerate(out_refs):
        own, other = load(own_ref.at[me ^ step]), load(other_ref.at[me ^ step])
        store(out_ref, choose(first, own, other), choose(first, other, own))


def read_scalars(refs, scalar_ref, me, slot):
    for step, ref in enumerate(refs):
        scalar_ref[0, pl.ds(me ^ step, 1), :] = tail_row(ref, TOP, slot)
        scalar_ref[1, pl.ds(me ^ step, 1), :] = tail_row(ref, DECAY, slot)
    count = len(refs)
    tops = [scalar_ref[0, place : place + 1, :] for place in range(count)]
    decays = [scalar_ref[1, place : place + 1, :] for place in range(count)]
    return tops, decays


def weights_of(tops, decays):
    moved, total = [], jnp.zeros_like(decays[0])
    for top, decay in zip(reversed(tops), reversed(decays)):
        moved.append(top + total)
        total = total + decay
    moved.reverse()
    joined = functools.reduce(jnp.maximum, moved)
    return [jnp.exp(top - joined) for top in moved], joined, total


def weighted_sum(weights, states):
    matrix, vector = 0.0, 0.0
    for weight, state in zip(weights, states):
        matrix = matrix + weight * state[0]
        vector = vector + weight * state[1]
    return matrix, vector


def quad_kernel(*refs):
    *refs, out_ref, scalar_ref = refs
    me = member(len(refs))
    totals = []
    for slot in range(SIDES):
        scalars = scalar_ref.at[slot]
        weights, top, decay = weights_of(*read_scalars(refs, scalars, me, slot))
        for place, weight in enumerate(weights):
            scalars[2, place : place + 1, :] = weight
        weights = [scalars[2, pl.ds(me ^ step, 1), :] for step in range(len(refs))]
        totals.append((*weighted_sum(weights, [load(ref, slot, SIDES) for ref in refs]), top, decay))
    store(out_ref, *totals)


def later_side(axis, bit):
    return (lax.axis_index(axis) & bit) != 0


def extend(is_later, other, before):
    return choose(is_later, join(other, before), before)


def butterfly_kernel(axis, bit, slots, *refs):
    total_ref, other_ref, *before_refs, out_total, out_before = refs
    is_later = later_side(axis, bit)
    totals, befores = [], []
    for slot in range(slots):
        total, other = load(total_ref, slot, slots), load(other_ref, slot, slots)
        before = load(before_refs[0], slot, slots) if before_refs else nothing(total)
        totals.append(join(choose(is_later, other, total), choose(is_later, total, other)))
        befores.append(extend(is_later, other, before))
    store(out_total, *totals)
    store(out_before, *befores)


def pair_kernel(in_ref, out_ref):
    store(out_ref, join(*(load(in_ref, slot, SIDES) for slot in range(SIDES))))


def prefix_kernel(axis, bit, quad, other_ref, group_ref, within_ref, *refs):
    *refs, scalar_ref, weight_ref = refs
    first = len(refs) - 2 * quad
    before_refs, pieces, out_refs = refs[:first], refs[first : first + quad], refs[first + quad :]
    me = member(quad)
    other = load(other_ref)
    before = load(before_refs[0]) if before_refs else nothing(other)
    start = extend(later_side(axis, bit), other, before)
    results = [[] for _ in range(quad)]
    for slot in range(SIDES):
        at_quad = join(start, load(within_ref, slot, SIDES))
        scalars, kept = scalar_ref.at[slot], weight_ref.at[slot]
        tops, decays = read_scalars(pieces, scalars, me, slot)
        zero = jnp.zeros_like(tops[0])
        for place in range(quad):
            weights, joined, _ = weights_of([at_quad[2]] + tops[:place], [zero] + decays[:place])
            weights += [zero] * (quad - place)
            for index, weight in enumerate(weights):
                kept[place, index : index + 1, :] = weight
            scalars[2, place : place + 1, :] = joined
        states = [at_quad] + [load(piece, slot, SIDES) for piece in pieces]
        for step in range(quad):
            place = me ^ step
            weights = [kept[place, 0:1, :]]
            weights += [kept[place, pl.ds(1 + (me ^ index), 1), :] for index in range(quad)]
            top = scalars[2, pl.ds(place, 1), :]
            results[step].append((*weighted_sum(weights, states), top, zero))
        start = join(start, load(group_ref, slot, SIDES))
    for out_ref, states in zip(out_refs, results):
        store(out_ref, *states)


def part_kernel(*refs):
    _, *refs, out_ref = refs
    key_dim = (refs[0].shape[0] - TAIL) // SIDES
    me, other = member(len(refs)), SIDES - 1 - own_side()
    for step, ref in enumerate(refs):
        out_ref[me ^ step] = ref[pl.ds(pl.multiple_of(other * key_dim, 8), key_dim), :]


def carry(query, matrix):
    high, low = split_two(matrix)
    return dot(jnp.concatenate([query, query], axis=1), jnp.concatenate([high, low], axis=0))


CUMUL, ROW_LEVEL, INNER_DEN = range(3)


def inner_kernel(q_ref, k_ref, v_ref, in_ref, fo_ref, num_ref, stat_ref):
    heads, length = in_ref.shape
    key_dim = q_ref.shape[1] // heads
    value_dim = v_ref.shape[1] // heads
    parts = value_dim // LANES
    logf = log_forget(fo_ref[...])
    level = in_ref[...] - cumulative_rows(logf)
    cumul = cumulative_columns(logf)
    causal = triangle(length, True)
    for head in range(heads):
        queries = q_ref[:, head * key_dim : (head + 1) * key_dim]
        keys = k_ref[:, head * key_dim : (head + 1) * key_dim]
        values = v_ref[:, head * value_dim : (head + 1) * value_dim]
        scores = dot_last(queries, keys) * (key_dim**-0.5)
        masked = jnp.where(causal, level[head : head + 1, :], -jnp.inf)
        row_level = jnp.max(masked, axis=1, keepdims=True)
        weighted = jnp.exp(masked - row_level) * scores
        stat_ref[head, :, CUMUL : CUMUL + 1] = cumul[:, head : head + 1]
        stat_ref[head, :, ROW_LEVEL : ROW_LEVEL + 1] = row_level
        stat_ref[head, :, INNER_DEN : INNER_DEN + 1] = jnp.sum(weighted, axis=1, keepdims=True)
        inner_num = dot(weighted.astype(jnp.bfloat16), values)
        for part in range(parts):
            num_ref[part, head] = inner_num[:, part * LANES : (part + 1) * LANES]


def outer_kernel(q_ref, num_ref, stat_ref, *refs):
    *refs, out_ref, factor_ref = refs
    heads = len(refs)
    key_dim = q_ref.shape[1] // heads
    scaling = key_dim**-0.5
    me, side = member(heads), own_side()
    for step, ref in enumerate(refs):
        head = me ^ step
        query = q_ref[:, pl.ds(pl.multiple_of(head * key_dim, LANES), key_dim)]
        carried = carry(query, ref[pl.ds(pl.multiple_of(side * key_dim, 8), key_dim), :])
        stats = stat_ref[head]
        cumul, row_level, inner_den = (stats[:, place : place + 1] for place in range(3))
        top = tail_row(ref, TOP, side)[:, 0:1]
        carried_den = jnp.sum(
            query.astype(jnp.float32) * tail_row(ref, VECTOR, side), axis=1, keepdims=True
        )
        joined = jnp.maximum(row_level, top)
        inner_factor = jnp.exp(row_level - joined)
        outer_factor = jnp.exp(top - joined) * scaling
        denom = inner_factor * inner_den + outer_factor * carried_den
        inverse = 1.0 / jnp.maximum(jnp.abs(denom), jnp.exp(-(cumul + joined)))
        inner_factor, outer_factor = inner_factor * inverse, outer_factor * inverse
        out_ref[head] = inner_factor * num_ref[side, head] + outer_factor * carried
        factor_ref[head, :, 0:1] = inner_factor
        factor_ref[head, :, 1:2] = outer_factor


def last_kernel(q_ref, num_ref, factor_ref, own_ref, state_ref, out_hbm, out_ref, done):
    heads, key_dim = state_ref.shape[:2]
    value_dim = out_ref.shape[1] // heads
    other = SIDES - 1 - own_side()
    copies = []
    for head in range(heads):
        carried = carry(q_ref[:, head * key_dim : (head + 1) * key_dim], state_ref[head])
        factors = factor_ref[head]
        late = factors[:, 0:1] * num_ref[other, head] + factors[:, 1:2] * carried
        early = own_ref[head]
        place = pl.ds(head * value_dim, value_dim)
        out_ref[:, place] = jnp.concatenate(
            [jnp.where(other == 0, late, early), jnp.where(other == 0, early, late)], axis=1
        ).astype(out_ref.dtype)
        copy = pltpu.make_async_copy(out_ref.at[:, place], out_hbm.at[:, place], done.at[head])
        copy.start()
        copies.append(copy)
    for copy in copies:
        copy.wait()


def swap(array, axis, step):
    count = lax.axis_size(axis)
    return lax.ppermute(array, axis, [(place, place ^ step) for place in range(count)])


def exchange(pieces):
    return [pieces[0]] + [swap(pieces[step], AXES[1], step) for step in range(1, len(pieces))]


def on_device(groups, group_length, queries, key_vectors, value_vectors, input_gate, forget_gate):
    heads, length = input_gate.shape
    key_dim = queries.shape[1] // heads
    value_dim = value_vectors.shape[1] // heads
    params = pltpu.CompilerParams(vmem_limit_bytes=48 * 1024 * 1024)
    hbm = pl.BlockSpec(memory_space=pltpu.HBM)

    def shape(*dims):
        return jax.ShapeDtypeStruct(dims, jnp.float32)

    def call(kernel, out_shape, *arrays, scratch=()):
        return pl.pallas_call(
            kernel, out_shape=out_shape, scratch_shapes=scratch, compiler_params=params
        )(*arrays)

    single = shape(key_dim + TAIL, LANES)
    double = shape(SIDES * key_dim + TAIL, LANES)
    halves = shape(heads, key_dim + TAIL, LANES)
    scalars = pltpu.VMEM((SIDES, 3, heads, LANES), jnp.float32)
    output = jax.ShapeDtypeStruct((length, heads * value_dim), jnp.bfloat16)
    operands = (key_vectors, value_vectors, input_gate, forget_gate)

    def levels(axis, bit, size):
        while bit < size:
            yield axis, bit
            bit *= 2

    own, send = pl.pallas_call(
        state_kernel,
        out_shape=(halves, halves),
        in_specs=[hbm] * len(operands),
        scratch_shapes=[pltpu.VMEM(array.shape, array.dtype) for array in operands]
        + [pltpu.SemaphoreType.DMA((len(operands),))],
        compiler_params=params,
    )(*(pltpu.with_memory_space_constraint(array, pltpu.HBM) for array in operands))
    packed = call(pack_kernel, (double,) * heads, own, swap(send, AXES[0], 1))
    pieces = exchange(packed)
    inner_num, stats = call(
        inner_kernel,
        (shape(value_dim // LANES, heads, length, LANES), shape(heads, length, 3)),
        queries,
        *operands,
    )
    group = call(quad_kernel, double, *pieces, scratch=[scalars])
    within = []
    for axis, bit in levels(AXES[1], heads, group_length):
        kernel = functools.partial(butterfly_kernel, axis, bit, SIDES)
        group, *within = call(kernel, (double, double), group, swap(group, axis, bit), *within)
    total = call(pair_kernel, single, group)
    before = []
    *steps, last = levels(AXES[0], SIDES, groups)
    for axis, bit in steps:
        kernel = functools.partial(butterfly_kernel, axis, bit, 1)
        total, *before = call(kernel, (single, single), total, swap(total, axis, bit), *before)
    states = call(
        functools.partial(prefix_kernel, *last, heads),
        (double,) * heads,
        swap(total, *last),
        group,
        *within,
        *before,
        *pieces,
        scratch=[scalars, pltpu.VMEM((SIDES, heads, 1 + heads, LANES), jnp.float32)],
    )
    carried = exchange(states)
    half = call(part_kernel, shape(heads, key_dim, LANES), stats, *carried)
    other_half = swap(half, AXES[0], 1)
    columns, factors = call(
        outer_kernel,
        (shape(heads, length, LANES), shape(heads, length, 2)),
        queries,
        inner_num,
        stats,
        *carried,
    )
    return pl.pallas_call(
        last_kernel,
        out_shape=output,
        out_specs=hbm,
        scratch_shapes=[
            pltpu.VMEM(output.shape, output.dtype),
            pltpu.SemaphoreType.DMA((heads,)),
        ],
        compiler_params=params,
    )(queries, inner_num, factors, columns, other_half)


def solution(mesh):
    return jax.shard_map(
        functools.partial(on_device, mesh.shape["grp"], mesh.shape["seq"]),
        mesh=mesh,
        in_specs=(
            P(AXES, None),
            P(AXES, None),
            P(AXES, None),
            P(None, AXES),
            P(None, AXES),
        ),
        out_specs=P(AXES, None),
        check_vma=False,
    )
```

time: 48.8 us -> 38.5 us (0.79)
  blocking collectives: 24.2 us -> 0 us
  starting transfers between devices: 2.76 us -> 13.1 us
  waiting for transfers between devices: 16.1 us -> 20 us
    all_to_all x1 -> x0, blocking collectives: 24.2 us -> none  [on_device(): gathered = lax.all_to_all(own, AXES, 0, 0)]
    ppermute x0 -> x10, waiting for transfers between devices: none -> 20 us  [swap(): lax.ppermute(array, axis, [(place, place ^ step) for place in range(count)])]
    all_to_all x1 -> x0, waiting for transfers between devices: 16.1 us -> none  [on_device(): carried = lax.all_to_all(before, AXES, 0, 0)]
    ppermute x0 -> x10, starting transfers between devices: none -> 13.1 us  [swap(): lax.ppermute(array, axis, [(place, place ^ step) for place in range(count)])]
    all_to_all x1 -> x0, starting transfers between devices: 2.76 us -> none  [on_device(): carried = lax.all_to_all(before, AXES, 0, 0)]
    pallas_call x4 -> x10, Pallas kernels: 5.41 us -> 5.17 us  [the longest x8 2.8 us: call(): pl.pallas_call(kernel, out_shape=out_shape, scratch_shapes=scratch, compi...]
  transfers between devices with their start and end apart: 1 -> 10, of which waited for: 1 -> 10; matrix products, arithmetic and copies ran while one was open for 0% -> 0% of each run, Pallas kernels for 2% -> 6%
where the time goes in v3:
time: 38.5 us; the launch traced here: 38.4 us
  waiting for transfers between devices  20 us (52%)
  starting transfers between devices  13.1 us (34%)
  Pallas kernels  5.17 us (13%)
    ppermute x10, waiting for transfers between devices, swap(): lax.ppermute(array, axis, [(place, place ^ step) for place in range(count)])  20 us
    ppermute x10, starting transfers between devices, swap(): lax.ppermute(array, axis, [(place, place ^ step) for place in range(count)])  13.1 us
    pallas_call x8, Pallas kernels, call(): pl.pallas_call(kernel, out_shape=out_shape, scratch_shapes=scratch, compi...  2.8 us
    pallas_call x1, Pallas kernels, on_device(): pl.pallas_call(state_kernel, out_shape=(halves, halves), in_specs=[hbm] *...  1.44 us
    pallas_call x1, Pallas kernels, on_device(): pl.pallas_call(last_kernel, out_shape=output, out_specs=hbm, scratch_shap...  0.93 us
  transfers between devices with their start and end apart: 10, of which 10 were waited for; matrix products, arithmetic and copies ran while one was open for 0% of the time, Pallas kernels for 6%

profile of v3, /device:TPU:0, one launch (start us, length us, event | category | flops | bytes accessed | tf_op | source)
XLA Modules:
  0.0 38.4 jit_solution(8433178445111820895)
XLA Ops:
  0.0 1.4 %shard_map.56 = (f32[4,136,128]{2,1,0:T(8,128)S(1)}, f32[4,136,128]{2,1,0:T(8,128)S(1)}) custom-call(bf16[128,512]{1,0:T(8,128)(2,1)} %k_hbm.1, bf16[128,1024]{1,0:T(8,128)(2,1)} %v_hbm.1, f32[4,128]{1,0:T(4,128)} %in_hbm.1, f32[4,128]{1,0:T(4,128)} %fo_hbm.1), custom_call_target="tpu_custom_call" | custom-call | tf_op jit(solution)/shard_map/pallas_call | solution.py:391
  1.4 0.5 %collective-permute-start = (f32[4,136,128]{2,1,0:T(8,128)S(1)}, f32[4,136,128]{2,1,0:T(8,128)S(1)}, u32[]{:S(2)}, u32[]{:S(2)}) collective-permute-start(f32[4,136,128]{2,1,0:T(8,128)S(1)} %get-tuple-element.24), channel_id=1, source_target_pairs={{0,8},{8,0},{16,24},{24,16},{1,9},{9,1},{17,25},{25,17},{2,10},{10... | collective-permute-start | bytes 835592 | tf_op jit(solution)/shard_map/ppermute | solution.py:357
  2.0 1.2 %collective-permute-done.other_ref = f32[4,136,128]{2,1,0:T(8,128)S(1)} collective-permute-done((f32[4,136,128]{2,1,0:T(8,128)S(1)}, f32[4,136,128]{2,1,0:T(8,128)S(1)}, u32[]{:S(2)}, u32[]{:S(2)}) %collective-permute-start) | collective-permute-done | bytes 278560 | tf_op jit(solution)/shard_map/ppermute | solution.py:357
  3.2 3.0 %collective-permute-start.1 = (f32[264,128]{1,0:T(8,128)S(1)}, f32[264,128]{1,0:T(8,128)S(1)}, u32[]{:S(2)}, u32[]{:S(2)}) collective-permute-start(f32[264,128]{1,0:T(8,128)S(1)} %get-tuple-element.26), channel_id=1, source_target_pairs={{0,1},{1,0},{2,3},{3,2},{4,5},{5,4},{6,7},{7,6},{8,9},{9,8},{10,11... | collective-permute-start | bytes 405512 | tf_op jit(solution)/shard_map/ppermute | solution.py:357
  6.2 1.6 %collective-permute-start.2 = (f32[264,128]{1,0:T(8,128)S(1)}, f32[264,128]{1,0:T(8,128)S(1)}, u32[]{:S(2)}, u32[]{:S(2)}) collective-permute-start(f32[264,128]{1,0:T(8,128)S(1)} %get-tuple-element.27), channel_id=1, source_target_pairs={{0,2},{1,3},{2,0},{3,1},{4,6},{5,7},{6,4},{7,5},{8,10},{9,11},{10,... | collective-permute-start | bytes 405512 | tf_op jit(solution)/shard_map/ppermute | solution.py:357
  7.7 0.0 collective-permute-start.3
  7.7 2.3 %collective-permute-done.1.refs_1_ = f32[264,128]{1,0:T(8,128)S(1)} collective-permute-done((f32[264,128]{1,0:T(8,128)S(1)}, f32[264,128]{1,0:T(8,128)S(1)}, u32[]{:S(2)}, u32[]{:S(2)}) %collective-permute-start.1) | collective-permute-done | bytes 135200 | tf_op jit(solution)/shard_map/ppermute | solution.py:357
  10.0 2.6 %collective-permute-done.2.refs_2_ = f32[264,128]{1,0:T(8,128)S(1)} collective-permute-done((f32[264,128]{1,0:T(8,128)S(1)}, f32[264,128]{1,0:T(8,128)S(1)}, u32[]{:S(2)}, u32[]{:S(2)}) %collective-permute-start.2) | collective-permute-done | bytes 135200 | tf_op jit(solution)/shard_map/ppermute | solution.py:357
  12.6 1.6 %collective-permute-done.3.refs_3_ = f32[264,128]{1,0:T(8,128)S(1)} collective-permute-done((f32[264,128]{1,0:T(8,128)S(1)}, f32[264,128]{1,0:T(8,128)S(1)}, u32[]{:S(2)}, u32[]{:S(2)}) %collective-permute-start.3) | collective-permute-done | bytes 135200 | tf_op jit(solution)/shard_map/ppermute | solution.py:357
  14.2 0.1 shard_map.58.refs_0_
  14.3 2.8 %collective-permute-start.4 = (f32[264,128]{1,0:T(8,128)S(1)}, f32[264,128]{1,0:T(8,128)S(1)}, u32[]{:S(2)}, u32[]{:S(2)}) collective-permute-start(f32[264,128]{1,0:T(8,128)S(1)} %shard_map.58.refs_0_), channel_id=1, source_target_pairs={{0,4},{1,5},{2,6},{3,7},{4,0},{5,1},{6,2},{7,3},{8,12},{9,13},{10,... | collective-permute-start | bytes 405512 | tf_op jit(solution)/shard_map/ppermute | solution.py:357
  17.1 6.0 %collective-permute-done.4.refs_1_ = f32[264,128]{1,0:T(8,128)S(1)} collective-permute-done((f32[264,128]{1,0:T(8,128)S(1)}, f32[264,128]{1,0:T(8,128)S(1)}, u32[]{:S(2)}, u32[]{:S(2)}) %collective-permute-start.4) | collective-permute-done | bytes 135200 | tf_op jit(solution)/shard_map/ppermute | solution.py:357
  23.1 0.1 shard_map.59
  23.1 1.6 %collective-permute-start.5 = (f32[136,128]{1,0:T(8,128)S(1)}, f32[136,128]{1,0:T(8,128)S(1)}, u32[]{:S(2)}, u32[]{:S(2)}) collective-permute-start(f32[136,128]{1,0:T(8,128)S(1)} %shard_map.60), channel_id=1, source_target_pairs={{0,16},{8,24},{16,0},{24,8},{1,17},{9,25},{17,1},{25,9},{2,18},{10... | collective-permute-start | bytes 208904 | tf_op jit(solution)/shard_map/ppermute | solution.py:357
  24.8 2.8 %collective-permute-done.5.other_ref = f32[136,128]{1,0:T(8,128)S(1)} collective-permute-done((f32[136,128]{1,0:T(8,128)S(1)}, f32[136,128]{1,0:T(8,128)S(1)}, u32[]{:S(2)}, u32[]{:S(2)}) %collective-permute-start.5) | collective-permute-done | bytes 69664 | tf_op jit(solution)/shard_map/ppermute | solution.py:357
  27.5 0.0 copy-start
  27.5 0.0 copy-start.1
  27.5 0.0 copy-start.2
  27.5 0.3 shard_map.61
  27.8 0.0 copy-start.4
  27.8 0.0 copy-start.3
  27.8 1.3 %collective-permute-start.6 = (f32[264,128]{1,0:T(8,128)S(1)}, f32[264,128]{1,0:T(8,128)S(1)}, u32[]{:S(2)}, u32[]{:S(2)}) collective-permute-start(f32[264,128]{1,0:T(8,128)S(1)} %get-tuple-element.32), channel_id=1, source_target_pairs={{0,1},{1,0},{2,3},{3,2},{4,5},{5,4},{6,7},{7,6},{8,9},{9,8},{10,11... | collective-permute-start | bytes 405512 | tf_op jit(solution)/shard_map/ppermute | solution.py:357
  29.1 0.7 %collective-permute-start.7 = (f32[264,128]{1,0:T(8,128)S(1)}, f32[264,128]{1,0:T(8,128)S(1)}, u32[]{:S(2)}, u32[]{:S(2)}) collective-permute-start(f32[264,128]{1,0:T(8,128)S(1)} %get-tuple-element.33), channel_id=1, source_target_pairs={{0,2},{1,3},{2,0},{3,1},{4,6},{5,7},{6,4},{7,5},{8,10},{9,11},{10,... | collective-permute-start | bytes 405512 | tf_op jit(solution)/shard_map/ppermute | solution.py:357
  29.8 1.6 %collective-permute-start.8 = (f32[264,128]{1,0:T(8,128)S(1)}, f32[264,128]{1,0:T(8,128)S(1)}, u32[]{:S(2)}, u32[]{:S(2)}) collective-permute-start(f32[264,128]{1,0:T(8,128)S(1)} %get-tuple-element.34), channel_id=1, source_target_pairs={{0,3},{1,2},{2,1},{3,0},{4,7},{5,6},{6,5},{7,4},{8,11},{9,10},{10,... | collective-permute-start | bytes 405512 | tf_op jit(solution)/shard_map/ppermute | solution.py:357
  31.4 0.0 copy-done
  31.4 0.0 copy-done.1
  31.4 0.0 copy-done.2
  31.4 0.0 copy-done.4
  31.4 0.0 copy-done.3
  31.4 0.9 %shard_map.55 = (f32[2,4,128,128]{3,2,1,0:T(8,128)S(1)}, f32[4,128,3]{2,1,0:T(8,128)S(1)}) custom-call(bf16[128,512]{1,0:T(8,128)(2,1)S(1)} %copy-done, bf16[128,512]{1,0:T(8,128)(2,1)S(1)} %copy-done.2, bf16[128,1024]{1,0:T(8,128)(2,1)S(1)} %copy-done.1, f32[4,128]{1,0:T(4,128)S(1)} %copy-done.3, f32[4,128]{1,0:T(4,128)S(1)} %copy-done.4), custom_call_target="tpu_custom_call" | custom-call | tf_op jit(solution)/shard_map/pallas_call | solution.py:375
  32.3 1.8 %collective-permute-done.6.refs_1_.refs_2_ = f32[264,128]{1,0:T(8,128)S(1)} collective-permute-done((f32[264,128]{1,0:T(8,128)S(1)}, f32[264,128]{1,0:T(8,128)S(1)}, u32[]{:S(2)}, u32[]{:S(2)}) %collective-permute-start.6) | collective-permute-done | bytes 135200 | tf_op jit(solution)/shard_map/ppermute | solution.py:357
  34.1 0.1 collective-permute-done.7.refs_2_.refs_3_
  34.2 1.7 %collective-permute-done.8.refs_3_.refs_4_ = f32[264,128]{1,0:T(8,128)S(1)} collective-permute-done((f32[264,128]{1,0:T(8,128)S(1)}, f32[264,128]{1,0:T(8,128)S(1)}, u32[]{:S(2)}, u32[]{:S(2)}) %collective-permute-start.8) | collective-permute-done | bytes 135200 | tf_op jit(solution)/shard_map/ppermute | solution.py:357
  35.8 0.1 collective-permute-start.9
  35.9 1.4 %shard_map.62 = (f32[4,128,128]{2,1,0:T(8,128)S(1)}, f32[4,128,2]{2,1,0:T(8,128)S(1)}) custom-call(bf16[128,512]{1,0:T(8,128)(2,1)S(1)} %copy-done, f32[2,4,128,128]{3,2,1,0:T(8,128)S(1)} %get-tuple-element.21.num_ref, f32[4,128,3]{2,1,0:T(8,128)S(1)} %get-tuple-element.22.stat_ref.refs_0_, f32[264,128]{1,0:T(8,128)S(1)} %get-tuple-element.31.refs_0_.refs_1_, ...), custom_call_target="tpu_custom_call" | custom-call | tf_op jit(solution)/shard_map/pallas_call | solution.py:375
  37.3 0.1 collective-permute-done.9.state_ref
  37.4 0.9 %shard_map.64 = bf16[128,1024]{1,0:T(8,128)(2,1)} custom-call(bf16[128,512]{1,0:T(8,128)(2,1)S(1)} %copy-done, f32[2,4,128,128]{3,2,1,0:T(8,128)S(1)} %get-tuple-element.21.num_ref, f32[4,128,2]{2,1,0:T(8,128)S(1)} %get-tuple-element.35.factor_ref, f32[4,128,128]{2,1,0:T(8,128)S(1)} %get-tuple-element.36.own_ref, ...), custom_call_target="tpu_custom_call" | custom-call | tf_op jit(solution)/shard_map/pallas_call | solution.py:439
  (3 shorter events, 0.1 us)
Async XLA Ops:
  1.4 1.7 %collective-permute-start = (f32[4,136,128]{2,1,0:T(8,128)S(1)}, f32[4,136,128]{2,1,0:T(8,128)S(1)}, u32[]{:S(2)}, u32[]{:S(2)}) collective-permute-start(f32[4,136,128]{2,1,0:T(8,128)S(1)} %get-tuple-element.24), channel_id=1, source_target_pairs={{0,8},{8,0},{16,24},{24,16},{1,9},{9,1},{17,25},{25,17},{2,10},{10... | collective-permute-start | bytes 835592 | tf_op jit(solution)/shard_map/ppermute | solution.py:357
  3.2 6.8 %collective-permute-start.1 = (f32[264,128]{1,0:T(8,128)S(1)}, f32[264,128]{1,0:T(8,128)S(1)}, u32[]{:S(2)}, u32[]{:S(2)}) collective-permute-start(f32[264,128]{1,0:T(8,128)S(1)} %get-tuple-element.26), channel_id=1, source_target_pairs={{0,1},{1,0},{2,3},{3,2},{4,5},{5,4},{6,7},{7,6},{8,9},{9,8},{10,11... | collective-permute-start | bytes 405512 | tf_op jit(solution)/shard_map/ppermute | solution.py:357
  6.2 6.5 %collective-permute-start.2 = (f32[264,128]{1,0:T(8,128)S(1)}, f32[264,128]{1,0:T(8,128)S(1)}, u32[]{:S(2)}, u32[]{:S(2)}) collective-permute-start(f32[264,128]{1,0:T(8,128)S(1)} %get-tuple-element.27), channel_id=1, source_target_pairs={{0,2},{1,3},{2,0},{3,1},{4,6},{5,7},{6,4},{7,5},{8,10},{9,11},{10,... | collective-permute-start | bytes 405512 | tf_op jit(solution)/shard_map/ppermute | solution.py:357
  7.7 6.5 %collective-permute-start.3 = (f32[264,128]{1,0:T(8,128)S(1)}, f32[264,128]{1,0:T(8,128)S(1)}, u32[]{:S(2)}, u32[]{:S(2)}) collective-permute-start(f32[264,128]{1,0:T(8,128)S(1)} %get-tuple-element.28), channel_id=1, source_target_pairs={{0,3},{1,2},{2,1},{3,0},{4,7},{5,6},{6,5},{7,4},{8,11},{9,10},{10,... | collective-permute-start | bytes 405512 | tf_op jit(solution)/shard_map/ppermute | solution.py:357
  14.3 8.8 %collective-permute-start.4 = (f32[264,128]{1,0:T(8,128)S(1)}, f32[264,128]{1,0:T(8,128)S(1)}, u32[]{:S(2)}, u32[]{:S(2)}) collective-permute-start(f32[264,128]{1,0:T(8,128)S(1)} %shard_map.58.refs_0_), channel_id=1, source_target_pairs={{0,4},{1,5},{2,6},{3,7},{4,0},{5,1},{6,2},{7,3},{8,12},{9,13},{10,... | collective-permute-start | bytes 405512 | tf_op jit(solution)/shard_map/ppermute | solution.py:357
  23.1 4.4 %collective-permute-start.5 = (f32[136,128]{1,0:T(8,128)S(1)}, f32[136,128]{1,0:T(8,128)S(1)}, u32[]{:S(2)}, u32[]{:S(2)}) collective-permute-start(f32[136,128]{1,0:T(8,128)S(1)} %shard_map.60), channel_id=1, source_target_pairs={{0,16},{8,24},{16,0},{24,8},{1,17},{9,25},{17,1},{25,9},{2,18},{10... | collective-permute-start | bytes 208904 | tf_op jit(solution)/shard_map/ppermute | solution.py:357
  27.5 3.9 %copy-start = (bf16[128,512]{1,0:T(8,128)(2,1)S(1)}, bf16[128,512]{1,0:T(8,128)(2,1)}, u32[]{:S(2)}) copy-start(bf16[128,512]{1,0:T(8,128)(2,1)} %q_ref.5) | copy-start | bytes 393220
  27.5 3.9 %copy-start.1 = (bf16[128,1024]{1,0:T(8,128)(2,1)S(1)}, bf16[128,1024]{1,0:T(8,128)(2,1)}, u32[]{:S(2)}) copy-start(bf16[128,1024]{1,0:T(8,128)(2,1)} %v_hbm.1) | copy-start | bytes 786436
  27.5 3.9 %copy-start.2 = (bf16[128,512]{1,0:T(8,128)(2,1)S(1)}, bf16[128,512]{1,0:T(8,128)(2,1)}, u32[]{:S(2)}) copy-start(bf16[128,512]{1,0:T(8,128)(2,1)} %k_hbm.1) | copy-start | bytes 393220
  27.8 3.6 %copy-start.4 = (f32[4,128]{1,0:T(4,128)S(1)}, f32[4,128]{1,0:T(4,128)}, u32[]{:S(2)}) copy-start(f32[4,128]{1,0:T(4,128)} %fo_hbm.1) | copy-start | bytes 6148
  27.8 3.6 %copy-start.3 = (f32[4,128]{1,0:T(4,128)S(1)}, f32[4,128]{1,0:T(4,128)}, u32[]{:S(2)}) copy-start(f32[4,128]{1,0:T(4,128)} %in_hbm.1) | copy-start | bytes 6148
  27.8 6.2 %collective-permute-start.6 = (f32[264,128]{1,0:T(8,128)S(1)}, f32[264,128]{1,0:T(8,128)S(1)}, u32[]{:S(2)}, u32[]{:S(2)}) collective-permute-start(f32[264,128]{1,0:T(8,128)S(1)} %get-tuple-element.32), channel_id=1, source_target_pairs={{0,1},{1,0},{2,3},{3,2},{4,5},{5,4},{6,7},{7,6},{8,9},{9,8},{10,11... | collective-permute-start | bytes 405512 | tf_op jit(solution)/shard_map/ppermute | solution.py:357
  29.1 5.0 %collective-permute-start.7 = (f32[264,128]{1,0:T(8,128)S(1)}, f32[264,128]{1,0:T(8,128)S(1)}, u32[]{:S(2)}, u32[]{:S(2)}) collective-permute-start(f32[264,128]{1,0:T(8,128)S(1)} %get-tuple-element.33), channel_id=1, source_target_pairs={{0,2},{1,3},{2,0},{3,1},{4,6},{5,7},{6,4},{7,5},{8,10},{9,11},{10,... | collective-permute-start | bytes 405512 | tf_op jit(solution)/shard_map/ppermute | solution.py:357
  29.8 6.0 %collective-permute-start.8 = (f32[264,128]{1,0:T(8,128)S(1)}, f32[264,128]{1,0:T(8,128)S(1)}, u32[]{:S(2)}, u32[]{:S(2)}) collective-permute-start(f32[264,128]{1,0:T(8,128)S(1)} %get-tuple-element.34), channel_id=1, source_target_pairs={{0,3},{1,2},{2,1},{3,0},{4,7},{5,6},{6,5},{7,4},{8,11},{9,10},{10,... | collective-permute-start | bytes 405512 | tf_op jit(solution)/shard_map/ppermute | solution.py:357
  35.8 1.6 %collective-permute-start.9 = (f32[4,128,128]{2,1,0:T(8,128)S(1)}, f32[4,128,128]{2,1,0:T(8,128)S(1)}, u32[]{:S(2)}, u32[]{:S(2)}) collective-permute-start(f32[4,128,128]{2,1,0:T(8,128)S(1)} %shard_map.63), channel_id=1, source_target_pairs={{0,8},{8,0},{16,24},{24,16},{1,9},{9,1},{17,25},{25,17},{2,10},{10... | collective-permute-start | bytes 786440 | tf_op jit(solution)/shard_map/ppermute | solution.py:357
